TPU v7x, 128 devices: a whole 4x4x4 slice. The times are simulated.
128 devices in a mesh: wide: 8 (over z, core), narrow: 16 (over y, x).
Axes of the slice: x: 4, y: 4, z: 4, core: 2. Of those that a mesh axis runs over, the one named last changes fastest.
Arguments:
- amplitudes: float32 [1024, 39936], P('wide', 'narrow'), may hold values from -6 to 6
- amp_tiles: int32 [16, 624], P('wide', 'narrow'), may hold values 0 or 1
- integrals: float32 [39936, 13312], P('narrow', 'wide'), may hold values from -0.03125 to 0.03125
- int_tiles: int32 [624, 208], P('narrow', 'wide'), may hold values 0 or 1
- cycle_weight: float32 [64, 4, 8], replicated, may hold values from -1 to 1
Outputs:
- cycle_term: float32 [64, 256, 1664], P(None, 'wide', 'narrow')
All inputs are finite; a program needn't handle non-finite values. No bound on the sum of `amp_tiles` or of `int_tiles` on one device may be relied on, other than what follows from the above.
Results may differ from a plain program's by a relative error of at most 0.000084.
Values sent between devices are 32-bit elements; how exact they have to be, the bound alone decides.
A program may use at most 192 MiB of HBM per device.

v0:
```python
import jax
import jax.numpy as jnp
from jax import lax
from jax.sharding import PartitionSpec as P

NV = 1664
NO = 256
TILE = 64
OI = 4


def expand(block, tiles):
    rows_t, cols_t = tiles.shape
    shaped = block.reshape(rows_t, TILE, cols_t, TILE) * tiles.astype(block.dtype)[:, None, :, None]
    return shaped.reshape(block.shape)


def shards(amplitudes, amp_tiles, integrals, int_tiles, cycle_weight):
    masked_amp = expand(amplitudes, amp_tiles)
    masked_int = expand(integrals, int_tiles)
    partial_value = jnp.dot(
        lax.all_gather(masked_amp, "wide", axis=0, tiled=True),
        masked_int,
        precision=lax.Precision.HIGHEST,
        preferred_element_type=jnp.float32,
    )
    local_a = partial_value.shape[1] // NV
    partial_value = partial_value.reshape(OI, NO, local_a, NV)
    reduced = lax.psum_scatter(partial_value, "narrow", scatter_dimension=3, tiled=True)
    regrouped = lax.all_to_all(reduced, "wide", split_axis=1, concat_axis=2, tiled=True)
    return jnp.einsum("kia,ijab->kjb", cycle_weight, regrouped, precision=lax.Precision.HIGHEST)


def solution(mesh):
    placed = (
        P("wide", "narrow"),
        P("wide", "narrow"),
        P("narrow", "wide"),
        P("narrow", "wide"),
        P(),
    )
    return jax.shard_map(
        shards, mesh=mesh, in_specs=placed, out_specs=P(None, "wide", "narrow"), check_vma=False
    )
```

profile of v0, /device:TPU:1, one launch (start us, length us, event | category | flops | bytes accessed | tf_op | source)
XLA Modules:
  0.0 317.4 jit_solution(14605149716105023739)
XLA Ops:
  6.5 0.0 copy-start
  6.5 0.0 copy-start.1
  6.5 0.0 all-gather.2.cloned.1.call-start
  6.5 0.7 convert_element_type.6
  7.2 0.1 copy.35
  7.4 0.7 mul.22
  8.1 2.5 mul.23
  10.6 2.9 mul.24
  13.4 0.0 all-gather.2.cloned.1.call-update
  13.5 0.0 all-reduce.3.cloned.1.call-start
  13.5 0.0 copy-done.1
  13.5 11.4 %mul.25 = f32[39,64,26,64]{1,0,3,2:T(8,128)} broadcast(f32[39,26]{0,1:T(8,128)S(1)} %convert_element_type.7), dimensions={0,2} | broadcast | bytes 16617432 | tf_op jit(solution)/shard_map/mul | solution.py:14
  24.9 26.6 %mul.26 = f32[2496,1664]{0,1:T(8,128)} reshape(f32[39,64,26,64]{1,0,3,2:T(8,128)} %mul.25) | data formatting | bytes 33226752 | tf_op jit(solution)/shard_map/mul | solution.py:14
  51.5 18.9 %copy.37 = f32[2496,1664]{1,0:T(8,128)} copy(f32[2496,1664]{0,1:T(8,128)} %mul.26) | data formatting | bytes 33226752 | tf_op jit(solution)/shard_map/mul | solution.py:14
  70.4 8.9 %all-gather.2.cloned.1.call-done = f32[1024,2496]{0,1:T(8,128)} async-done(((f32[128,2496]{0,1:T(8,128)}), f32[1024,2496]{0,1:T(8,128)}) %all-gather.2.cloned.1.call-update) | async-done | bytes 10223632 | tf_op jit(solution)/shard_map/all_gather | solution.py:22
  79.3 11.2 %copy.36 = f32[1024,2496]{1,0:T(8,128)} copy(f32[1024,2496]{0,1:T(8,128)} %all-gather.2.cloned.1.call-done) | data formatting | bytes 20447232 | tf_op jit(solution)/shard_map/all_gather | solution.py:22
  90.5 65.5 %fusion.3 = f32[4,256,1,1664]{3,1,0,2:T(8,128)} fusion(f32[4,256,2496]{2,1,0:T(8,128)} %bitcast.32, f32[2496,1664]{1,0:T(8,128)} %param.7, f32[2496,1664]{1,0:T(8,128)} %copy.37), kind=kOutput, calls=%fused_computation.3 | convolution fusion | flops 51040444416 | bytes 50266112 | tf_op jit(solution)/shard_map/dot_general | solution.py:21
  155.9 0.0 copy-start.2
  156.0 8.8 %copy.39 = f32[4,256,1,1664]{1,0,2,3:T(4,128)} copy(f32[4,256,1,1664]{3,1,0,2:T(8,128)} %fusion.3) | data formatting | bytes 13631488 | tf_op jit(solution)/shard_map/dot_general | solution.py:21
  164.8 0.0 all-reduce.3.cloned.1.call-update
  164.8 0.0 copy-done.2
  164.8 0.6 dynamic-slice
  166.1 126.0 %all-reduce.3.cloned.1.call-done = f32[4,256,1,1664]{1,0,2,3:T(4,128)} async-done(((f32[4,256,1,1664]{1,0,2,3:T(4,128)}), f32[4,256,1,1664]{1,0,2,3:T(4,128)}) %all-reduce.3.cloned.1.call-update) | async-done | bytes 6815760
  292.1 1.0 constant_dynamic-slice_fusion
  293.1 0.3 copy.40
  293.4 14.3 %all_to_all.18 = f32[4,256,1,104]{3,0,2,1:T(4,128)S(1)} all-to-all(f32[4,256,1,104]{3,0,2,1:T(4,128)S(1)} %copy.40), channel_id=1, replica_groups=mesh['wide'=8,'narrow'=16] {'wide'}, dimensions={1} | all-to-all | bytes 851968 | tf_op jit(solution)/shard_map/all_to_all | solution.py:30
  307.7 0.0 copy-done
  307.7 1.3 convolution_bitcast_fusion
  309.0 1.6 copy.43
  (1 shorter events, 0.0 us)
Async XLA Ops:
  6.5 301.1 %copy-start = (f32[64,4,8]{0,2,1:T(8,128)S(1)}, f32[64,4,8]{0,2,1:T(8,128)}, u32[]{:S(2)}) copy-start(f32[64,4,8]{0,2,1:T(8,128)} %param.9) | copy-start | bytes 24580
  6.5 7.0 %copy-start.1 = (s32[39,26]{0,1:T(8,128)S(1)}, s32[39,26]{0,1:T(8,128)}, u32[]{:S(2)}) copy-start(s32[39,26]{0,1:T(8,128)} %param.8) | copy-start | bytes 12172
  6.5 72.8 %all-gather.2.cloned.1.call-start = ((), (), s32[]{:S(2)}) async-start(), calls=%async_computation.1 | async-start | bytes 11501568 | tf_op jit(solution)/shard_map/all_gather | solution.py:22
  13.5 278.7 %all-reduce.3.cloned.1.call-start = ((), (), s32[]{:S(2)}) async-start(), calls=%async_computation.2 | async-start | bytes 13631488
  155.9 8.9 %copy-start.2 = (u32[128]{0:T(128)S(1)}, u32[128]{0:T(128)}, u32[]{:S(2)}) copy-start(u32[128]{0:T(128)} %constant.4) | copy-start | bytes 1540
Sparse Core Ops, SparseCore 0:
  13.6 65.7 all-gather.1
  164.9 127.1 all-reduce.2
where the time goes:
time: 319 us; the launch traced here: 317 us
  waiting for transfers between devices  135 us (42%)
  local copies, waits for them, and re-layouts  83.6 us (26%)
  matrix products  66.8 us (21%)
  blocking collectives  14.3 us (4%)
  between operations  14.1 us (4%)
  other arithmetic  3.59 us (1%)
    unnamed x3, waiting for transfers between devices  126 us
    dot_general x1, matrix products, shards(): jnp.dot(lax.all_gather(masked_amp, 'wide', axis=0, tiled=True), masked_in...  65.5 us
    mul x5, local copies, waits for them, and re-layouts, expand(): block.reshape(rows_t, TILE, cols_t, TILE)  60.1 us
    all_to_all x1, blocking collectives, shards(): lax.all_to_all(reduced, 'wide', split_axis=1, concat_axis=2, tiled=True)  14.3 us
    all_gather x1, local copies, waits for them, and re-layouts, shards(): lax.all_gather(masked_amp, 'wide', axis=0, tiled=True)  11.2 us
    all_gather x1, waiting for transfers between devices, shards(): lax.all_gather(masked_amp, 'wide', axis=0, tiled=True)  8.92 us
    dot_general x1, local copies, waits for them, and re-layouts, shards(): jnp.dot(lax.all_gather(masked_amp, 'wide', axis=0, tiled=True), masked_in...  8.85 us
  transfers between devices with their start and end apart: 2, of which 2 were waited for; matrix products, arithmetic and copies ran while one was open for 18% of the time, Pallas kernels for 0%

commit v1 on v0

v1 whole, which is shorter than its diff:
```python
import functools

import jax
import jax.numpy as jnp
from jax import lax
from jax.experimental import pallas as pl
from jax.experimental.pallas import tpu as pltpu
from jax.sharding import PartitionSpec as P

MESH = pl.DeviceIdType.MESH
F32 = jnp.float32
BF16 = jnp.bfloat16
TILE = 64
K = 2496
KP = 2560
KB = 256
NK = KP // KB
M = 1664
PIECE = 104
CUT = 56
CHUNK = 4 * PIECE
OFF = (2, 1, 3, 0)
NT = (((1,), (1,)), ((), ()))


def dot_nt(a, b):
    return lax.dot_general(a, b, NT, preferred_element_type=F32)


def split(value):
    high = value.astype(BF16)
    return high, (value - high.astype(F32)).astype(BF16)


def spread(flags, columns):
    tiles = flags.shape[1]
    row = lax.broadcasted_iota(jnp.int32, (tiles, columns), 0)
    lane = lax.broadcasted_iota(jnp.int32, (tiles, columns), 1)
    pick = jnp.where(lane // TILE == row, 1.0, 0.0).astype(BF16)
    return jnp.dot(flags.astype(F32).astype(BF16), pick, preferred_element_type=F32)


def kernel(
    amp, amp_tiles, ints, int_tiles, weight, out,
    amp_in, int_in, amps, flags, int_hi, int_lo, amp_hi, amp_lo, part,
    r1, r2, r3, r4, turned, regrouped, w_hi, w_lo,
    load_sem, z_send, z_recv, c_send, c_recv, s_send, s_recv, a_send, a_recv,
):
    wide, narrow = lax.axis_index("wide"), lax.axis_index("narrow")
    z, core = wide // 2, wide % 2
    y, x = narrow // 4, narrow % 4

    def at_z(step):
        return (((z + step) % 4) * 2 + core, narrow)

    def at_x(step):
        return (wide, y * 4 + (x + step) % 4)

    def at_y(step):
        return (wide, ((y + step) % 4) * 4 + x)

    sibling = (z * 2 + 1 - core, narrow)

    load_amp = pltpu.make_async_copy(amp, amp_in, load_sem.at[2])
    load_amp.start()

    def load_int(step, slot):
        return pltpu.make_async_copy(ints.at[pl.ds(step * KB, KB)], int_in.at[slot], load_sem.at[slot])

    rest = K - (NK - 1) * KB
    load_last = pltpu.make_async_copy(
        ints.at[pl.ds((NK - 1) * KB, rest)], int_in.at[(NK - 1) % 2, pl.ds(0, rest)], load_sem.at[(NK - 1) % 2]
    )
    load_int(0, 0).start()
    load_int(1, 1).start()

    barrier = pltpu.get_barrier_semaphore()
    for step in range(1, 8):
        pl.semaphore_signal(barrier, inc=1, device_id=((wide + step) % 8, narrow), device_id_type=MESH)
    for device in (at_x(1), at_x(3), at_y(1), at_y(3)):
        pl.semaphore_signal(barrier, inc=1, device_id=device, device_id_type=MESH)

    amp_flags = spread(amp_tiles[...], K)
    load_amp.wait()
    half_rows = [pl.ds(pl.multiple_of(h * 128 + core * 64, 64), 64) for h in range(2)]
    for h in range(2):
        amps[0, half_rows[h], pl.ds(0, K)] = amp_in[pl.ds(h * 64, 64), :] * amp_flags[h : h + 1, :]
        amps[0, half_rows[h], pl.ds(K, KP - K)] = jnp.zeros((64, KP - K), F32)
    pl.semaphore_wait(barrier, 11)

    sent = []

    def send(src, dst, send_sem, recv_sem, device):
        copy = pltpu.make_async_remote_copy(
            src_ref=src, dst_ref=dst, send_sem=send_sem, recv_sem=recv_sem, device_id=device, device_id_type=MESH
        )
        return copy

    def z_copy(index):
        step, kind = (1, index) if index < 3 else (3, index - 3)
        side = 0 if index < 3 else 1
        if kind < 2:
            src = amps.at[0, half_rows[(kind + side) % 2]]
        else:
            src = amps.at[1, half_rows[side]]
        return send(src, amps.at[kind + 1, half_rows[side]], z_send.at[index], z_recv.at[index], at_z(step))

    def c_copy(block, side):
        ref = amps.at[block, half_rows[side]]
        return send(ref, ref, c_send.at[block, side], c_recv.at[block, side], sibling)

    zs = [z_copy(i) for i in range(6)]
    cs = [[c_copy(b, s) for s in range(2)] for b in range(4)]
    for i in (0, 3):
        zs[i].start()
    for s in range(2):
        cs[0][s].start()
    for i in (1, 4):
        zs[i].start()

    int_flags = spread(int_tiles[...], M)
    for step in range(NK):
        count = min(4, K // TILE - step * 4)
        flags[step, pl.ds(0, count), :] = int_flags[step * 4 : step * 4 + count, :]

    def prepare(step, slot, rows):
        for half in range(2):
            for col in range(M // 128):
                cols = pl.ds(col * 128, 128)
                parts = []
                for t in range(2):
                    first = half * 128 + t * 64
                    if first < rows:
                        flag = flags[step, pl.ds(half * 2 + t, 1), cols]
                        parts.append(int_in[slot, pl.ds(first, 64), cols] * flag)
                    else:
                        parts.append(jnp.zeros((64, 128), F32))
                high, low = split(jnp.concatenate(parts, axis=0).T)
                int_hi[step, cols, pl.ds(half * 128, 128)] = high
                int_lo[step, cols, pl.ds(half * 128, 128)] = low

    def prepare_step(step, _):
        slot = step % 2
        load_int(step, slot).wait()
        prepare(step, slot, KB)

        @pl.when(step + 2 < NK - 1)
        def _():
            load_int(step + 2, slot).start()

        @pl.when(step + 2 == NK - 1)
        def _():
            load_last.start()

        return 0

    lax.fori_loop(0, NK - 1, prepare_step, 0)
    load_last.wait()
    prepare(NK - 1, (NK - 1) % 2, rest)

    def spread_weight(piece):
        r = lax.broadcasted_iota(jnp.int32, (512, 64), 0)
        c = lax.broadcasted_iota(jnp.int32, (512, 64), 1)
        rows = jnp.where(r // 8 == c, 1.0, 0.0).astype(BF16)
        r2_ = lax.broadcasted_iota(jnp.int32, (8, 64), 0)
        c2_ = lax.broadcasted_iota(jnp.int32, (8, 64), 1)
        cols = jnp.where(c2_ // 8 == r2_, 1.0, 0.0).astype(BF16)
        wide_piece = jnp.dot(piece, cols, preferred_element_type=F32).astype(BF16)
        tall = jnp.dot(rows, wide_piece, preferred_element_type=F32)
        return jnp.where(r % 8 == c % 8, tall, 0.0).astype(BF16)

    for i in range(4):
        high, low = split(weight[:, i, :])
        w_hi[:, pl.ds(i * 64, 64)] = spread_weight(high)
        w_lo[:, pl.ds(i * 64, 64)] = spread_weight(low)

    along = ((at_x, at_y), (at_y, at_x))

    def place(half, ra, rb):
        first, second = (x, y) if half == 0 else (y, x)
        pa, pb = (first + ra) % 4, (second + rb) % 4
        py, px = (pb, pa) if half == 0 else (pa, pb)
        return pl.ds(pl.multiple_of(py * CHUNK + px * PIECE, 8), PIECE)

    def off(r):
        if isinstance(r, int):
            return OFF[r]
        return jnp.where(r == 0, 2, jnp.where(r == 1, 1, jnp.where(r == 2, 3, 0)))

    def cols_of(half):
        return pl.ds(half * 128, 128)

    def s1p1(q, half, rb):
        step = (1 if rb < 2 else 3) if isinstance(rb, int) else jnp.where(rb < 2, 1, 3)
        src = part.at[q, place(half, 2, off(rb)), cols_of(half)]
        return send(src, r1.at[q, half, rb], s_send.at[q, half, rb], s_recv.at[q, half, rb], along[half][0](step))

    def s1p2(q, half, side, rb):
        step = (1 + 2 * side) if isinstance(side, int) else jnp.where(side == 0, 1, 3)
        src = part.at[q, place(half, step, off(rb)), cols_of(half)]
        index = 4 + side * 4 + rb
        return send(
            src, r2.at[q, half, side, rb], s_send.at[q, half, index], s_recv.at[q, half, index], along[half][0](step)
        )

    def s2_rows(side):
        return (0, CUT) if side == 0 else (CUT, PIECE - CUT)

    def s2p1(q, half, side):
        start, size = s2_rows(side)
        whole = place(half, 0, 2)
        rows = pl.ds(pl.multiple_of(whole.start + start, 8), size)
        index = 12 + side
        return send(
            part.at[q, rows, cols_of(half)], r3.at[q, half, side, pl.ds(0, size)],
            s_send.at[q, half, index], s_recv.at[q, half, index], along[half][1](1 + 2 * side),
        )

    def s2p2(q, half, side):
        step = 1 + 2 * side
        index = 14 + side
        return send(
            part.at[q, place(half, 0, step), cols_of(half)], r4.at[q, half, side],
            s_send.at[q, half, index], s_recv.at[q, half, index], along[half][1](step),
        )

    def after_chunk(q, ry):
        near = jnp.where(ry < 2, 1, 0)
        s1p1(q, 0, ry).start()
        s1p2(q, 0, near, ry).start()

        @pl.when(ry == 0)
        def _():
            for rb in range(4):
                s1p1(q, 1, rb).start()

        for side in range(2):

            @pl.when(ry == 1 + side)
            def _():
                for rb in (2, 3) if side == 0 else (0, 1):
                    s1p2(q, 1, side, rb).start()

    def first_sums(q):
        for half in range(2):
            for rb in range(4):
                side = 0 if rb < 2 else 1
                s1p1(q, half, rb).wait_recv()
                rows = place(half, 1 + 2 * side, off(rb))
                part[q, rows, cols_of(half)] += r1[q, half, rb]
                s1p2(q, half, side, rb).start()

    def own_sums(q):
        for rb in range(4):
            for half in range(2):
                for side in range(2):
                    s1p2(q, half, side, rb).wait_recv()
                part[q, place(half, 0, off(rb)), cols_of(half)] += r2[q, half, 0, rb] + r2[q, half, 1, rb]
                if rb == 0:
                    for side in range(2):
                        s2p1(q, half, side).start()

    def second_sums(q):
        for half in range(2):
            for side in range(2):
                s2p1(q, half, side).wait_recv()
                start, size = s2_rows(side)
                whole = place(half, 0, 1 + 2 * side)
                rows = pl.ds(pl.multiple_of(whole.start + start, 8), size)
                part[q, rows, cols_of(half)] += r3[q, half, side, pl.ds(0, size)]
                s2p2(q, half, side).start()

    def group(q, dest):
        dc, dh, dl = dest // 4, (dest // 2) % 2, dest % 2
        if q == 0:
            return dh * 4 + dc * 2 + dl, z
        if q == 1:
            return dh * 4 + dc * 2 + dl, (z + 3 + 2 * dh) % 4
        if q == 2:
            return (1 - dh) * 4 + dc * 2 + dl, (z + 1 + 2 * dh) % 4
        return dh * 4 + dc * 2 + dl, (z + 2) % 4

    def regroup(q, step):
        dest = (wide + step) % 8
        position, i = group(q, dest)
        src = turned.at[q, pl.ds(pl.multiple_of(position * 32, 32), 32)]
        return send(src, regrouped.at[i, wide], a_send.at[q, step], a_recv.at[q, step], (dest, narrow))

    def last_sums(q):
        for half in range(2):
            for side in range(2):
                s2p2(q, half, side).wait_recv()
            total = part[q, place(half, 0, 0), cols_of(half)] + r4[q, half, 0] + r4[q, half, 1]
            total = jnp.concatenate([total, jnp.zeros((128 - PIECE, 128), F32)], axis=0)
            turned[q, cols_of(half), :] = total.T
        for step in range(1, 8):
            regroup(q, step).start()
        position, i = group(q, wide)
        regrouped[i, wide] = turned[q, pl.ds(pl.multiple_of(position * 32, 32), 32), :]

    def multiply(q):
        for k in range(NK):
            high, low = split(amps[q, :, pl.ds(k * KB, KB)])
            amp_hi[k] = high
            amp_lo[k] = low

        def chunk(ry, _):
            rows = pl.ds(pl.multiple_of(((y + off(ry)) % 4) * CHUNK, 8), CHUNK)
            total = None
            for k in range(NK):
                term = dot_nt(int_hi[k, rows], amp_hi[k]) + dot_nt(int_hi[k, rows], amp_lo[k])
                term = term + dot_nt(int_lo[k, rows], amp_hi[k])
                total = term if total is None else total + term
            part[q, rows, :] = total
            after_chunk(q, ry)
            if q > 0:

                @pl.when(ry == 0)
                def _():
                    second_sums(q - 1)

                @pl.when(ry == 2)
                def _():
                    last_sums(q - 1)

            return 0

        lax.fori_loop(0, 4, chunk, 0)

    for q in range(4):
        if q > 0:
            for side in range(2):
                zs[3 * side + q - 1].wait_recv()
                cs[q][side].start()
                if q == 1:
                    zs[3 * side + 2].start()
        for side in range(2):
            cs[q][side].wait_recv()
        multiply(q)
        first_sums(q)
        own_sums(q)
    second_sums(3)
    last_sums(3)

    for q in range(4):
        for step in range(1, 8):
            regroup(q, step).wait_recv()
    for g in range(4):
        value = regrouped[:, :, pl.ds(g * 8, 8), :].reshape(256, 128)
        high, low = split(value)
        total = jnp.dot(w_hi[...], high, preferred_element_type=F32)
        total += jnp.dot(w_hi[...], low, preferred_element_type=F32)
        total += jnp.dot(w_lo[...], high, preferred_element_type=F32)
        out[:, pl.ds(g * 8, 8), :] = total.reshape(64, 8, 128)[:, :, :PIECE]

    for copy in zs:
        copy.wait_send()
    for block in cs:
        for copy in block:
            copy.wait_send()
    for q in range(4):
        for half in range(2):
            for rb in range(4):
                s1p1(q, half, rb).wait_send()
                for side in range(2):
                    s1p2(q, half, side, rb).wait_send()
            for side in range(2):
                s2p1(q, half, side).wait_send()
                s2p2(q, half, side).wait_send()
        for step in range(1, 8):
            regroup(q, step).wait_send()


def shards(amplitudes, amp_tiles, integrals, int_tiles, cycle_weight):
    vmem = pl.BlockSpec(memory_space=pltpu.VMEM)
    hbm = pl.BlockSpec(memory_space=pl.ANY)
    dma = pltpu.SemaphoreType.DMA
    return pl.pallas_call(
        kernel,
        out_shape=jax.ShapeDtypeStruct((64, 32, PIECE), F32),
        in_specs=[hbm, vmem, hbm, vmem, vmem],
        out_specs=vmem,
        scratch_shapes=[
            pltpu.VMEM((128, K), F32),
            pltpu.VMEM((2, KB, M), F32),
            pltpu.VMEM((4, 256, KP), F32),
            pltpu.VMEM((NK, 8, M), F32),
            pltpu.VMEM((NK, M, KB), BF16),
            pltpu.VMEM((NK, M, KB), BF16),
            pltpu.VMEM((NK, 256, KB), BF16),
            pltpu.VMEM((NK, 256, KB), BF16),
            pltpu.VMEM((4, M, 256), F32),
            pltpu.VMEM((4, 2, 4, PIECE, 128), F32),
            pltpu.VMEM((4, 2, 2, 4, PIECE, 128), F32),
            pltpu.VMEM((4, 2, 2, CUT, 128), F32),
            pltpu.VMEM((4, 2, 2, PIECE, 128), F32),
            pltpu.VMEM((4, 256, 128), F32),
            pltpu.VMEM((4, 8, 32, 128), F32),
            pltpu.VMEM((512, 256), BF16),
            pltpu.VMEM((512, 256), BF16),
            dma((3,)),
            dma((6,)),
            dma((6,)),
            dma((4, 2)),
            dma((4, 2)),
            dma((4, 2, 16)),
            dma((4, 2, 16)),
            dma((4, 8)),
            dma((4, 8)),
        ],
        compiler_params=pltpu.CompilerParams(
            collective_id=0, has_side_effects=True, vmem_limit_bytes=60 * 1024 * 1024
        ),
        cost_estimate=pl.CostEstimate(
            flops=6 * 1024 * KP * M, bytes_accessed=4 * (K * M + 128 * K + 64 * 32 * 128), transcendentals=0
        ),
    )(amplitudes, amp_tiles, integrals, int_tiles, cycle_weight)


def solution(mesh):
    placed = (
        P("wide", "narrow"),
        P("wide", "narrow"),
        P("narrow", "wide"),
        P("narrow", "wide"),
        P(),
    )
    return jax.shard_map(
        shards, mesh=mesh, in_specs=placed, out_specs=P(None, "wide", "narrow"), check_vma=False
    )
```

time: 319 us -> 119 us (0.37)
  waiting for transfers between devices: 135 us -> 0 us
  Pallas kernels: 0 us -> 111 us
  local copies, waits for them, and re-layouts: 83.6 us -> 7.9 us
  matrix products: 66.8 us -> 0 us
  blocking collectives: 14.3 us -> 0 us
  between operations: 14.1 us -> 0.01 us
  other arithmetic: 3.59 us -> 0 us
    unnamed x3 -> x0, waiting for transfers between devices: 126 us -> none
    pallas_call x0 -> x1, Pallas kernels: none -> 111 us  [shards(): pl.pallas_call(kernel, out_shape=jax.ShapeDtypeStruct((64, 32, PIECE), F3...]
    dot_general x2 -> x0, matrix products: 66.8 us -> none  [the longest x1 65.5 us: shards(): jnp.dot(lax.all_gather(masked_amp, 'wide', axis=0, tiled=True), masked_in...]
    mul x5 -> x0, local copies, waits for them, and re-layouts: 60.1 us -> none  [expand(): block.reshape(rows_t, TILE, cols_t, TILE)]
    all_to_all x1 -> x0, blocking collectives: 14.3 us -> none  [shards(): lax.all_to_all(reduced, 'wide', split_axis=1, concat_axis=2, tiled=True)]
    all_gather x1 -> x0, local copies, waits for them, and re-layouts: 11.2 us -> none  [shards(): lax.all_gather(masked_amp, 'wide', axis=0, tiled=True)]
    dot_general x2 -> x0, local copies, waits for them, and re-layouts: 10.4 us -> none  [the longest x1 8.85 us: shards(): jnp.dot(lax.all_gather(masked_amp, 'wide', axis=0, tiled=True), masked_in...]
    all_gather x1 -> x0, waiting for transfers between devices: 8.92 us -> none  [shards(): lax.all_gather(masked_amp, 'wide', axis=0, tiled=True)]
  transfers between devices with their start and end apart: 2 -> 0, of which waited for: 2 -> 0; matrix products, arithmetic and copies ran while one was open for 18% -> 0% of each run, Pallas kernels for 0% -> 0%
where the time goes in v1:
time: 119 us
  Pallas kernels  111 us (93%)
  local copies, waits for them, and re-layouts  7.9 us (7%)
    pallas_call x1, Pallas kernels, shards(): pl.pallas_call(kernel, out_shape=jax.ShapeDtypeStruct((64, 32, PIECE), F3...  111 us
    unnamed x4, local copies, waits for them, and re-layouts  7.9 us

profile of v1, /device:TPU:1, one launch (start us, length us, event | category | flops | bytes accessed | tf_op | source)
XLA Modules:
  0.0 118.8 jit_solution(17111721703037480874)
XLA Ops:
  0.0 1.4 %copy.7.int_tiles = s32[39,26]{1,0:T(8,128)} copy(s32[39,26]{0,1:T(8,128)} %param.8) | data formatting | bytes 8112 | tf_op args[3]
  1.4 1.5 %copy.8.weight = f32[64,4,8]{2,1,0:T(4,128)} copy(f32[64,4,8]{0,2,1:T(8,128)} %param.9) | data formatting | bytes 16384 | tf_op args[4]
  2.9 2.8 %copy.6.amp = f32[128,2496]{1,0:T(8,128)} copy(f32[128,2496]{0,1:T(8,128)} %param.5) | data formatting | bytes 2555904 | tf_op args[0]
  5.6 110.9 %shard_map.55 = f32[64,32,104]{2,1,0:T(8,128)} custom-call(f32[128,2496]{1,0:T(8,128)} %copy.6.amp, s32[2,39]{1,0:T(2,128)} %amp_tiles.1, f32[2496,1664]{1,0:T(8,128)} %ints.1, s32[39,26]{1,0:T(8,128)} %copy.7.int_tiles, f32[64,4,8]{2,1,0:T(4,128)} %copy.8.weight), custom_call_target="tpu_custom_call" | custom-call | flops 26172456960 | bytes 18939904 | tf_op jit(solution)/shard_map/pallas_call | solution.py:378
  116.5 2.3 %copy.10 = f32[64,32,104]{2,1,0:T(8,128)} copy(f32[64,32,104]{2,1,0:T(8,128)} %shard_map.55) | data formatting | bytes 1703936

commit v2 on v1

v2 whole, which is shorter than its diff:
```python
import functools

import jax
import jax.numpy as jnp
from jax import lax
from jax.experimental import pallas as pl
from jax.experimental.pallas import tpu as pltpu
from jax.sharding import PartitionSpec as P

MESH = pl.DeviceIdType.MESH
F32 = jnp.float32
BF16 = jnp.bfloat16
TILE = 64
K = 2496
KP = 2560
KB = 256
NK = KP // KB
M = 1664
PIECE = 104
CHUNK = 4 * PIECE
CUT = 56
LAST = 3
SPLIT = 6
CUTS = (pl.ds(0, SPLIT * KB), pl.ds(SPLIT * KB, KP - SPLIT * KB))
OFF = (2, 1, 3, 0)
NT = (((1,), (1,)), ((), ()))


def dot_nt(a, b):
    return lax.dot_general(a, b, NT, preferred_element_type=F32)


def split(value):
    high = value.astype(BF16)
    return high, (value - high.astype(F32)).astype(BF16)


def pick(tiles, columns):
    row = lax.broadcasted_iota(jnp.int32, (tiles, columns), 0)
    lane = lax.broadcasted_iota(jnp.int32, (tiles, columns), 1)
    return jnp.where(lane // TILE == row, 1.0, 0.0).astype(BF16)


def kernel(
    amp, amp_tiles, ints, int_tiles, weight, out,
    amp_in, int_in, amps, flags, int_hi, int_lo, amp_hi, amp_lo, part,
    r1, r2, r3, r4, r5, r6, turned, regrouped, w_hi, w_lo,
    load_sem, z_send, z_recv, c_send, c_recv, s_send, s_recv, a_send, a_recv,
):
    wide, narrow = lax.axis_index("wide"), lax.axis_index("narrow")
    z, core = wide // 2, wide % 2
    y, x = narrow // 4, narrow % 4

    def at_z(step):
        return (((z + step) % 4) * 2 + core, narrow)

    def at_x(step):
        return (wide, y * 4 + (x + step) % 4)

    def at_y(step):
        return (wide, ((y + step) % 4) * 4 + x)

    sibling = (z * 2 + 1 - core, narrow)

    load_amp = pltpu.make_async_copy(amp, amp_in, load_sem.at[2])
    load_amp.start()

    def load_int(step, slot):
        return pltpu.make_async_copy(ints.at[pl.ds(step * KB, KB)], int_in.at[slot], load_sem.at[slot])

    rest = K - (NK - 1) * KB
    load_last = pltpu.make_async_copy(
        ints.at[pl.ds((NK - 1) * KB, rest)], int_in.at[(NK - 1) % 2, pl.ds(0, rest)], load_sem.at[(NK - 1) % 2]
    )
    load_int(0, 0).start()
    load_int(1, 1).start()

    barrier = pltpu.get_barrier_semaphore()
    for step in range(1, 8):
        pl.semaphore_signal(barrier, inc=1, device_id=((wide + step) % 8, narrow), device_id_type=MESH)
    for device in (at_x(1), at_x(3), at_y(1), at_y(3)):
        pl.semaphore_signal(barrier, inc=1, device_id=device, device_id_type=MESH)

    amp_flags = amp_tiles[...].astype(F32).astype(BF16)
    amp_flags = jnp.dot(amp_flags, pick(K // TILE, KP), preferred_element_type=F32)
    load_amp.wait()
    half_rows = [pl.ds(pl.multiple_of(h * 128 + core * 64, 64), 64) for h in range(2)]
    for step in range(KP // 128):
        first = step * 128
        value = amp_in[pl.ds(first, min(128, K - first)), :]
        if first + 128 > K:
            value = jnp.concatenate([value, jnp.zeros((first + 128 - K, 128), F32)], axis=0)
        value = value.T
        for h in range(2):
            flag = amp_flags[h : h + 1, first : first + 128]
            amps[0, half_rows[h], pl.ds(first, 128)] = value[h * 64 : h * 64 + 64, :] * flag
    pl.semaphore_wait(barrier, 11)

    def send(src, dst, send_sem, recv_sem, device):
        copy = pltpu.make_async_remote_copy(
            src_ref=src, dst_ref=dst, send_sem=send_sem, recv_sem=recv_sem, device_id=device, device_id_type=MESH
        )
        return copy

    def z_copy(side, kind, cut):
        src, dst = (0, (kind + side) % 2) if kind < 2 else (1, side), (kind + 1, side)
        index = (side * 3 + kind) * 2 + cut
        return send(
            amps.at[src[0], half_rows[src[1]], CUTS[cut]], amps.at[dst[0], half_rows[dst[1]], CUTS[cut]],
            z_send.at[index], z_recv.at[index], at_z(1 + 2 * side),
        )

    def c_copy(block, side, cut):
        ref = amps.at[block, half_rows[side], CUTS[cut]]
        index = (block * 2 + side) * 2 + cut
        return send(ref, ref, c_send.at[index], c_recv.at[index], sibling)

    def start_z(kind):
        for cut in range(2):
            for side in range(2):
                z_copy(side, kind, cut).start()

    def swap(block, cut):
        for side in range(2):
            z_copy(side, block - 1, cut).wait_recv()
            c_copy(block, side, cut).start()

    def have(block, cut):
        for side in range(2):
            c_copy(block, side, cut).wait_recv()

    start_z(0)
    for cut in range(2):
        for side in range(2):
            c_copy(0, side, cut).start()
    start_z(1)

    int_flags = int_tiles[...].astype(F32).astype(BF16)
    int_flags = lax.dot_general(int_flags, pick(M // TILE, M), (((0,), (0,)), ((), ())), preferred_element_type=F32)
    for step in range(NK):
        count = min(4, K // TILE - step * 4)
        flags[step, pl.ds(0, count), :] = int_flags[step * 4 : step * 4 + count, :]

    def prepare(step, slot, rows):
        for half in range(2):
            for col in range(M // 128):
                cols = pl.ds(col * 128, 128)
                parts = []
                for t in range(2):
                    first = half * 128 + t * 64
                    if first < rows:
                        flag = flags[step, pl.ds(half * 2 + t, 1), cols]
                        parts.append(int_in[slot, pl.ds(first, 64), cols] * flag)
                    else:
                        parts.append(jnp.zeros((64, 128), F32))
                high, low = split(jnp.concatenate(parts, axis=0).T)
                int_hi[step, cols, pl.ds(half * 128, 128)] = high
                int_lo[step, cols, pl.ds(half * 128, 128)] = low

    def prepare_step(step, _):
        slot = step % 2
        load_int(step, slot).wait()
        prepare(step, slot, KB)

        @pl.when(step + 2 < NK - 1)
        def _():
            load_int(step + 2, slot).start()

        @pl.when(step + 2 == NK - 1)
        def _():
            load_last.start()

        return 0

    lax.fori_loop(0, NK - 1, prepare_step, 0)
    load_last.wait()
    prepare(NK - 1, (NK - 1) % 2, rest)

    def spread_weight(piece):
        r = lax.broadcasted_iota(jnp.int32, (512, 64), 0)
        c = lax.broadcasted_iota(jnp.int32, (512, 64), 1)
        rows = jnp.where(r // 8 == c, 1.0, 0.0).astype(BF16)
        from_a = lax.broadcasted_iota(jnp.int32, (8, 64), 0)
        to_a = lax.broadcasted_iota(jnp.int32, (8, 64), 1) // 8
        columns = jnp.where(from_a == to_a, 1.0, 0.0).astype(BF16)
        tall = dot_nt(rows, piece).astype(BF16)
        return jnp.where(r % 8 == c % 8, jnp.dot(tall, columns, preferred_element_type=F32), 0.0).astype(BF16)

    for i in range(4):
        high, low = split(weight[i])
        w_hi[:, pl.ds(i * 64, 64)] = spread_weight(high)
        w_lo[:, pl.ds(i * 64, 64)] = spread_weight(low)

    along = ((at_x, at_y), (at_y, at_x))

    def place(half, ra, rb):
        first, second = (x, y) if half == 0 else (y, x)
        pa, pb = (first + ra) % 4, (second + rb) % 4
        py, px = (pb, pa) if half == 0 else (pa, pb)
        return pl.ds(pl.multiple_of(py * CHUNK + px * PIECE, 8), PIECE)

    def off(r):
        if isinstance(r, int):
            return OFF[r]
        return jnp.where(r == 0, 2, jnp.where(r == 1, 1, jnp.where(r == 2, 3, 0)))

    def cols_of(half):
        return pl.ds(half * 128, 128)

    def rows_of(ry):
        return pl.ds(pl.multiple_of(((y + off(ry)) % 4) * CHUNK, 8), CHUNK)

    def first_copy(q, ra, rb):
        src = part.at[q, place(0, off(ra), off(rb)), cols_of(0)]
        index = ra * 4 + rb
        return send(
            src, r1.at[0, ra, pl.ds(rb * PIECE, PIECE)], s_send.at[q, 0, index], s_recv.at[q, 0, index],
            at_x(off(ra)),
        )

    def first_copy_rows(q, ra):
        return send(
            part.at[q, rows_of(ra), cols_of(1)], r1.at[1, ra], s_send.at[q, 1, ra], s_recv.at[q, 1, ra],
            at_y(off(ra)),
        )

    def second_copy(q, half, rb):
        src = part.at[q, place(half, 0, off(rb)), cols_of(half)]
        index = 12 + rb
        return send(
            src, r2.at[half, rb], s_send.at[q, half, index], s_recv.at[q, half, index], along[half][1](off(rb))
        )

    def s1p1(q, half, rb):
        step = (1 if rb < 2 else 3) if isinstance(rb, int) else jnp.where(rb < 2, 1, 3)
        src = part.at[q, place(half, 2, off(rb)), cols_of(half)]
        return send(src, r3.at[q, half, rb], s_send.at[q, half, rb], s_recv.at[q, half, rb], along[half][0](step))

    def s1p2(q, half, side, rb):
        step = (1 + 2 * side) if isinstance(side, int) else jnp.where(side == 0, 1, 3)
        src = part.at[q, place(half, step, off(rb)), cols_of(half)]
        index = 4 + side * 4 + rb
        return send(
            src, r4.at[q, half, side, rb], s_send.at[q, half, index], s_recv.at[q, half, index], along[half][0](step)
        )

    def s2_rows(side):
        return (0, CUT) if side == 0 else (CUT, PIECE - CUT)

    def s2p1(q, half, side):
        start, size = s2_rows(side)
        whole = place(half, 0, 2)
        rows = pl.ds(pl.multiple_of(whole.start + start, 8), size)
        index = 12 + side
        return send(
            part.at[q, rows, cols_of(half)], r5.at[q, half, side, pl.ds(0, size)],
            s_send.at[q, half, index], s_recv.at[q, half, index], along[half][1](1 + 2 * side),
        )

    def s2p2(q, half, side):
        step = 1 + 2 * side
        index = 14 + side
        return send(
            part.at[q, place(half, 0, step), cols_of(half)], r6.at[q, half, side],
            s_send.at[q, half, index], s_recv.at[q, half, index], along[half][1](step),
        )

    def ring_after_chunk(q, ry):
        near = jnp.where(ry < 2, 1, 0)
        s1p1(q, 0, ry).start()
        s1p2(q, 0, near, ry).start()

        @pl.when(ry == 0)
        def _():
            for rb in range(4):
                s1p1(q, 1, rb).start()

        for side in range(2):

            @pl.when(ry == 1 + side)
            def _():
                for rb in (2, 3) if side == 0 else (0, 1):
                    s1p2(q, 1, side, rb).start()

    def pass_on(q, half, rb):
        side = 0 if rb < 2 else 1
        s1p1(q, half, rb).wait_recv()
        rows = place(half, 1 + 2 * side, off(rb))
        part[q, rows, cols_of(half)] += r3[q, half, rb]
        s1p2(q, half, side, rb).start()

    def ring_own_sum(q, half, rb):
        for side in range(2):
            s1p2(q, half, side, rb).wait_recv()
        part[q, place(half, 0, off(rb)), cols_of(half)] += r4[q, half, 0, rb] + r4[q, half, 1, rb]
        if rb == 0:
            for side in range(2):
                s2p1(q, half, side).start()

    def pass_on_second(q, half, side):
        s2p1(q, half, side).wait_recv()
        start, size = s2_rows(side)
        whole = place(half, 0, 1 + 2 * side)
        rows = pl.ds(pl.multiple_of(whole.start + start, 8), size)
        part[q, rows, cols_of(half)] += r5[q, half, side, pl.ds(0, size)]
        s2p2(q, half, side).start()

    def after_chunk(q, ry):
        if q < LAST:
            ring_after_chunk(q, ry)
            return

        @pl.when(ry < 3)
        def _():
            first_copy_rows(q, ry).start()

        for ra in range(3):
            first_copy(q, ra, ry).start()

    def ring_own_sums(q):
        for rb in range(4):
            for half in (1, 0):
                ring_own_sum(q, half, rb)

    def pass_all(q):
        for rb in range(4):
            for half in (1, 0):
                pass_on(q, half, rb)

    def second_sums(q):
        for half in (1, 0):
            for side in range(2):
                pass_on_second(q, half, side)

    def own_sums(q):
        for ra in range(3):
            first_copy_rows(q, ra).wait_recv()
        for rb in range(4):
            for half in (1, 0):
                if half == 0:
                    for ra in range(3):
                        first_copy(q, ra, rb).wait_recv()
                    here = [pl.ds(rb * PIECE, PIECE)] * 3
                else:
                    here = [pl.ds(pl.multiple_of(((x + off(rb)) % 4) * PIECE, 8), PIECE)] * 3
                total = part[q, place(half, 0, off(rb)), cols_of(half)]
                for ra in range(3):
                    total = total + r1[half, ra, here[ra]]
                part[q, place(half, 0, off(rb)), cols_of(half)] = total
                if rb < 3:
                    second_copy(q, half, rb).start()

    def group(q, dest):
        dc, dh, dl = dest // 4, (dest // 2) % 2, dest % 2
        if q == 0:
            return dh * 4 + dc * 2 + dl, z
        if q == 1:
            return dh * 4 + dc * 2 + dl, (z + 3 + 2 * dh) % 4
        if q == 2:
            return (1 - dh) * 4 + dc * 2 + dl, (z + 1 + 2 * dh) % 4
        return dh * 4 + dc * 2 + dl, (z + 2) % 4

    def regroup(q, step):
        dest = (wide + step) % 8
        position, i = group(q, dest)
        src = turned.at[q, pl.ds(pl.multiple_of(position * 32, 32), 32)]
        return send(src, regrouped.at[i, wide], a_send.at[q, step], a_recv.at[q, step], (dest, narrow))

    def last_sum(q, half):
        total = part[q, place(half, 0, 0), cols_of(half)]
        if q < LAST:
            for side in range(2):
                s2p2(q, half, side).wait_recv()
            total = total + r6[q, half, 0] + r6[q, half, 1]
        else:
            for rb in range(3):
                second_copy(q, half, rb).wait_recv()
                total = total + r2[half, rb]
        total = jnp.concatenate([total, jnp.zeros((128 - PIECE, 128), F32)], axis=0)
        turned[q, cols_of(half), :] = total.T

    def hand_out(q):
        for step in range(1, 8):
            regroup(q, step).start()
        position, i = group(q, wide)
        regrouped[i, wide] = turned[q, pl.ds(pl.multiple_of(position * 32, 32), 32), :]

    def last_sums(q):
        for half in (1, 0):
            last_sum(q, half)
        hand_out(q)

    def split_block(q, steps):
        for k in steps:
            high, low = split(amps[q, :, pl.ds(k * KB, KB)])
            amp_hi[k] = high
            amp_lo[k] = low

    def product(rows, steps):
        total = None
        for k in steps:
            term = dot_nt(int_hi[k, rows], amp_hi[k]) + dot_nt(int_hi[k, rows], amp_lo[k])
            term = term + dot_nt(int_lo[k, rows], amp_hi[k])
            total = term if total is None else total + term
        return total

    def multiply_first(q, steps, slots):
        split_block(q, steps)

        def chunk(ry, _):
            rows = rows_of(ry)
            part[q, rows, :] = product(rows, steps)
            for at, action in slots:
                pl.when(ry == at)(action)
            return 0

        lax.fori_loop(0, 4, chunk, 0)

    def multiply(q, steps, slots):
        split_block(q, steps)

        def chunk(ry, _):
            rows = rows_of(ry)
            total = product(rows, steps)
            part[q, rows, :] = total if len(steps) == NK else part[q, rows, :] + total
            after_chunk(q, ry)

            for at, action in slots:
                pl.when(ry == at)(action)
            return 0

        lax.fori_loop(0, 4, chunk, 0)

    every = range(NK)
    front, back = every[:SPLIT], every[SPLIT:]
    have(0, 0)
    have(0, 1)
    multiply(0, every, ((2, lambda: swap(1, 0)),))
    have(1, 0)
    multiply_first(1, front, ((1, lambda: swap(1, 1)), (3, lambda: pass_all(0))))
    start_z(2)
    have(1, 1)
    multiply(1, back, ())
    ring_own_sums(0)
    swap(2, 0)
    have(2, 0)
    multiply_first(2, front, (
        (0, lambda: pass_all(1)), (1, lambda: second_sums(0)), (2, lambda: swap(2, 1)),
    ))
    have(2, 1)
    multiply(2, back, ((0, lambda: ring_own_sums(1)), (2, lambda: last_sums(0))))
    second_sums(1)
    swap(3, 0)
    pass_all(2)
    have(3, 0)
    multiply_first(3, front, ((1, lambda: last_sums(1)),))
    swap(3, 1)
    ring_own_sums(2)
    have(3, 1)
    multiply(3, back, ((3, lambda: second_sums(2)),))
    own_sums(3)
    last_sums(2)
    last_sums(3)

    for q in range(4):
        for step in range(1, 8):
            regroup(q, step).wait_recv()
    for g in range(4):
        value = regrouped[:, :, pl.ds(g * 8, 8), :].reshape(256, 128)
        high, low = split(value)
        total = jnp.dot(w_hi[...], high, preferred_element_type=F32)
        total += jnp.dot(w_hi[...], low, preferred_element_type=F32)
        total += jnp.dot(w_lo[...], high, preferred_element_type=F32)
        out[:, pl.ds(g * 8, 8), :] = total.reshape(64, 8, 128)[:, :, :PIECE]

    for side in range(2):
        for cut in range(2):
            for kind in range(3):
                z_copy(side, kind, cut).wait_send()
            for block in range(4):
                c_copy(block, side, cut).wait_send()
    for q in range(4):
        if q < LAST:
            for half in range(2):
                for rb in range(4):
                    s1p1(q, half, rb).wait_send()
                    for side in range(2):
                        s1p2(q, half, side, rb).wait_send()
                for side in range(2):
                    s2p1(q, half, side).wait_send()
                    s2p2(q, half, side).wait_send()
        else:
            for half in range(2):
                for rb in range(3):
                    second_copy(q, half, rb).wait_send()
            for ra in range(3):
                first_copy_rows(q, ra).wait_send()
                for rb in range(4):
                    first_copy(q, ra, rb).wait_send()
        for step in range(1, 8):
            regroup(q, step).wait_send()


def shards(amplitudes, amp_tiles, integrals, int_tiles, cycle_weight):
    vmem = pl.BlockSpec(memory_space=pltpu.VMEM)
    hbm = pl.BlockSpec(memory_space=pl.ANY)
    dma = pltpu.SemaphoreType.DMA
    return pl.pallas_call(
        kernel,
        out_shape=jax.ShapeDtypeStruct((64, 32, PIECE), F32),
        in_specs=[hbm, vmem, hbm, vmem, vmem],
        out_specs=vmem,
        scratch_shapes=[
            pltpu.VMEM((K, 128), F32),
            pltpu.VMEM((2, KB, M), F32),
            pltpu.VMEM((4, 256, KP), F32),
            pltpu.VMEM((NK, 8, M), F32),
            pltpu.VMEM((NK, M, KB), BF16),
            pltpu.VMEM((NK, M, KB), BF16),
            pltpu.VMEM((NK, 256, KB), BF16),
            pltpu.VMEM((NK, 256, KB), BF16),
            pltpu.VMEM((4, M, 256), F32),
            pltpu.VMEM((2, 3, CHUNK, 128), F32),
            pltpu.VMEM((2, 3, PIECE, 128), F32),
            pltpu.VMEM((LAST, 2, 4, PIECE, 128), F32),
            pltpu.VMEM((LAST, 2, 2, 4, PIECE, 128), F32),
            pltpu.VMEM((LAST, 2, 2, CUT, 128), F32),
            pltpu.VMEM((LAST, 2, 2, PIECE, 128), F32),
            pltpu.VMEM((4, 256, 128), F32),
            pltpu.VMEM((4, 8, 32, 128), F32),
            pltpu.VMEM((512, 256), BF16),
            pltpu.VMEM((512, 256), BF16),
            dma((3,)),
            dma((12,)),
            dma((12,)),
            dma((16,)),
            dma((16,)),
            dma((4, 2, 16)),
            dma((4, 2, 16)),
            dma((4, 8)),
            dma((4, 8)),
        ],
        compiler_params=pltpu.CompilerParams(
            collective_id=0, has_side_effects=True, vmem_limit_bytes=60 * 1024 * 1024
        ),
        cost_estimate=pl.CostEstimate(
            flops=6 * 1024 * KP * M, bytes_accessed=4 * (K * M + 128 * K + 64 * 32 * 128), transcendentals=0
        ),
    )(amplitudes.T, amp_tiles, integrals, int_tiles.T, cycle_weight.transpose(1, 2, 0))


def solution(mesh):
    placed = (
        P("wide", "narrow"),
        P("wide", "narrow"),
        P("narrow", "wide"),
        P("narrow", "wide"),
        P(),
    )
    return jax.shard_map(
        shards, mesh=mesh, in_specs=placed, out_specs=P(None, "wide", "narrow"), check_vma=False
    )
```

time: 119 us -> 90.1 us (0.76)
  Pallas kernels: 111 us -> 87.5 us
  local copies, waits for them, and re-layouts: 7.9 us -> 2.26 us
    pallas_call x1, Pallas kernels: 111 us -> 87.5 us  [shards(): pl.pallas_call(kernel, out_shape=jax.ShapeDtypeStruct((64, 32, PIECE), F3...]
    unnamed x4 -> x1, local copies, waits for them, and re-layouts: 7.9 us -> 2.26 us
where the time goes in v2:
time: 90.1 us; the launch traced here: 89.8 us
  Pallas kernels  87.5 us (97%)
  local copies, waits for them, and re-layouts  2.26 us (3%)
    pallas_call x1, Pallas kernels, shards(): pl.pallas_call(kernel, out_shape=jax.ShapeDtypeStruct((64, 32, PIECE), F3...  87.5 us
    unnamed x1, local copies, waits for them, and re-layouts  2.26 us

profile of v2, /device:TPU:1, one launch (start us, length us, event | category | flops | bytes accessed | tf_op | source)
XLA Modules:
  0.0 89.8 jit_solution(6229889523219711451)
XLA Ops:
  0.0 87.5 %shard_map.55 = f32[64,32,104]{2,1,0:T(8,128)} custom-call(f32[2496,128]{1,0:T(8,128)} %bitcast.3, s32[2,39]{1,0:T(2,128)} %amp_tiles.1, f32[2496,1664]{1,0:T(8,128)} %ints.1, s32[26,39]{1,0:T(8,128)} %bitcast.4, f32[4,8,64]{2,1,0:T(8,128)} %bitcast.5), custom_call_target="tpu_custom_call" | custom-call | flops 26172456960 | bytes 18939904 | tf_op jit(solution)/shard_map/pallas_call | solution.py:508
  87.5 2.3 %copy.7 = f32[64,32,104]{2,1,0:T(8,128)} copy(f32[64,32,104]{2,1,0:T(8,128)} %shard_map.55) | data formatting | bytes 1703936

commit v3 on v2

--- a/solution.py
+++ b/solution.py
@@ -18,7 +18,6 @@
 M = 1664
 PIECE = 104
 CHUNK = 4 * PIECE
-CUT = 56
 LAST = 3
 SPLIT = 6
 CUTS = (pl.ds(0, SPLIT * KB), pl.ds(SPLIT * KB, KP - SPLIT * KB))
@@ -44,7 +43,7 @@
 def kernel(
     amp, amp_tiles, ints, int_tiles, weight, out,
     amp_in, int_in, amps, flags, int_hi, int_lo, amp_hi, amp_lo, part,
-    r1, r2, r3, r4, r5, r6, turned, regrouped, w_hi, w_lo,
+    r1, r2, r3, r4, turned, regrouped, w_hi, w_lo,
     load_sem, z_send, z_recv, c_send, c_recv, s_send, s_recv, a_send, a_recv,
 ):
     wide, narrow = lax.axis_index("wide"), lax.axis_index("narrow")
@@ -85,16 +84,16 @@
     amp_flags = jnp.dot(amp_flags, pick(K // TILE, KP), preferred_element_type=F32)
     load_amp.wait()
     half_rows = [pl.ds(pl.multiple_of(h * 128 + core * 64, 64), 64) for h in range(2)]
-    for step in range(KP // 128):
-        first = step * 128
-        value = amp_in[pl.ds(first, min(128, K - first)), :]
-        if first + 128 > K:
-            value = jnp.concatenate([value, jnp.zeros((first + 128 - K, 128), F32)], axis=0)
-        value = value.T
-        for h in range(2):
-            flag = amp_flags[h : h + 1, first : first + 128]
-            amps[0, half_rows[h], pl.ds(first, 128)] = value[h * 64 : h * 64 + 64, :] * flag
-    pl.semaphore_wait(barrier, 11)
+    def mask(steps):
+        for step in steps:
+            first = step * 128
+            value = amp_in[pl.ds(first, min(128, K - first)), :]
+            if first + 128 > K:
+                value = jnp.concatenate([value, jnp.zeros((first + 128 - K, 128), F32)], axis=0)
+            value = value.T
+            for h in range(2):
+                flag = amp_flags[h : h + 1, first : first + 128]
+                amps[0, half_rows[h], pl.ds(first, 128)] = value[h * 64 : h * 64 + 64, :] * flag
 
     def send(src, dst, send_sem, recv_sem, device):
         copy = pltpu.make_async_remote_copy(
@@ -129,8 +128,11 @@
         for side in range(2):
             c_copy(block, side, cut).wait_recv()
 
-    start_z(0)
+    mask(range(KP // 128))
+    pl.semaphore_wait(barrier, 11)
     for cut in range(2):
+        for side in range(2):
+            z_copy(side, 0, cut).start()
         for side in range(2):
             c_copy(0, side, cut).start()
     start_z(1)
@@ -228,7 +230,7 @@
         src = part.at[q, place(half, 0, off(rb)), cols_of(half)]
         index = 12 + rb
         return send(
-            src, r2.at[half, rb], s_send.at[q, half, index], s_recv.at[q, half, index], along[half][1](off(rb))
+            src, r2.at[q, half, rb], s_send.at[q, half, index], s_recv.at[q, half, index], along[half][1](off(rb))
         )
 
     def s1p1(q, half, rb):
@@ -244,27 +246,6 @@
             src, r4.at[q, half, side, rb], s_send.at[q, half, index], s_recv.at[q, half, index], along[half][0](step)
         )
 
-    def s2_rows(side):
-        return (0, CUT) if side == 0 else (CUT, PIECE - CUT)
-
-    def s2p1(q, half, side):
-        start, size = s2_rows(side)
-        whole = place(half, 0, 2)
-        rows = pl.ds(pl.multiple_of(whole.start + start, 8), size)
-        index = 12 + side
-        return send(
-            part.at[q, rows, cols_of(half)], r5.at[q, half, side, pl.ds(0, size)],
-            s_send.at[q, half, index], s_recv.at[q, half, index], along[half][1](1 + 2 * side),
-        )
-
-    def s2p2(q, half, side):
-        step = 1 + 2 * side
-        index = 14 + side
-        return send(
-            part.at[q, place(half, 0, step), cols_of(half)], r6.at[q, half, side],
-            s_send.at[q, half, index], s_recv.at[q, half, index], along[half][1](step),
-        )
-
     def ring_after_chunk(q, ry):
         near = jnp.where(ry < 2, 1, 0)
         s1p1(q, 0, ry).start()
@@ -293,17 +274,8 @@
         for side in range(2):
             s1p2(q, half, side, rb).wait_recv()
         part[q, place(half, 0, off(rb)), cols_of(half)] += r4[q, half, 0, rb] + r4[q, half, 1, rb]
-        if rb == 0:
-            for side in range(2):
-                s2p1(q, half, side).start()
-
-    def pass_on_second(q, half, side):
-        s2p1(q, half, side).wait_recv()
-        start, size = s2_rows(side)
-        whole = place(half, 0, 1 + 2 * side)
-        rows = pl.ds(pl.multiple_of(whole.start + start, 8), size)
-        part[q, rows, cols_of(half)] += r5[q, half, side, pl.ds(0, size)]
-        s2p2(q, half, side).start()
+        if rb < 3:
+            second_copy(q, half, rb).start()
 
     def after_chunk(q, ry):
         if q < LAST:
@@ -326,11 +298,6 @@
         for rb in range(4):
             for half in (1, 0):
                 pass_on(q, half, rb)
-
-    def second_sums(q):
-        for half in (1, 0):
-            for side in range(2):
-                pass_on_second(q, half, side)
 
     def own_sums(q):
         for ra in range(3):
@@ -368,19 +335,14 @@
 
     def last_sum(q, half):
         total = part[q, place(half, 0, 0), cols_of(half)]
-        if q < LAST:
-            for side in range(2):
-                s2p2(q, half, side).wait_recv()
-            total = total + r6[q, half, 0] + r6[q, half, 1]
-        else:
-            for rb in range(3):
-                second_copy(q, half, rb).wait_recv()
-                total = total + r2[half, rb]
+        for rb in range(3):
+            second_copy(q, half, rb).wait_recv()
+            total = total + r2[q, half, rb]
         total = jnp.concatenate([total, jnp.zeros((128 - PIECE, 128), F32)], axis=0)
         turned[q, cols_of(half), :] = total.T
 
     def hand_out(q):
-        for step in range(1, 8):
+        for step in (4, 3, 5, 2, 6, 1, 7):
             regroup(q, step).start()
         position, i = group(q, wide)
         regrouped[i, wide] = turned[q, pl.ds(pl.multiple_of(position * 32, 32), 32), :]
@@ -441,25 +403,20 @@
     start_z(2)
     have(1, 1)
     multiply(1, back, ())
-    ring_own_sums(0)
     swap(2, 0)
     have(2, 0)
-    multiply_first(2, front, (
-        (0, lambda: pass_all(1)), (1, lambda: second_sums(0)), (2, lambda: swap(2, 1)),
-    ))
+    multiply_first(2, front, ((0, lambda: ring_own_sums(0)), (1, lambda: pass_all(1)), (2, lambda: swap(2, 1))))
     have(2, 1)
-    multiply(2, back, ((0, lambda: ring_own_sums(1)), (2, lambda: last_sums(0))))
-    second_sums(1)
+    multiply(2, back, ((1, lambda: last_sums(0)),))
+    ring_own_sums(1)
     swap(3, 0)
-    pass_all(2)
     have(3, 0)
-    multiply_first(3, front, ((1, lambda: last_sums(1)),))
+    multiply_first(3, front, ((0, lambda: pass_all(2)), (2, lambda: last_sums(1)),))
     swap(3, 1)
     ring_own_sums(2)
     have(3, 1)
-    multiply(3, back, ((3, lambda: second_sums(2)),))
+    multiply(3, back, ((3, lambda: last_sums(2)),))
     own_sums(3)
-    last_sums(2)
     last_sums(3)
 
     for q in range(4):
@@ -480,19 +437,16 @@
             for block in range(4):
                 c_copy(block, side, cut).wait_send()
     for q in range(4):
+        for half in range(2):
+            for rb in range(3):
+                second_copy(q, half, rb).wait_send()
         if q < LAST:
             for half in range(2):
                 for rb in range(4):
                     s1p1(q, half, rb).wait_send()
                     for side in range(2):
                         s1p2(q, half, side, rb).wait_send()
-                for side in range(2):
-                    s2p1(q, half, side).wait_send()
-                    s2p2(q, half, side).wait_send()
         else:
-            for half in range(2):
-                for rb in range(3):
-                    second_copy(q, half, rb).wait_send()
             for ra in range(3):
                 first_copy_rows(q, ra).wait_send()
                 for rb in range(4):
@@ -521,11 +475,9 @@
             pltpu.VMEM((NK, 256, KB), BF16),
             pltpu.VMEM((4, M, 256), F32),
             pltpu.VMEM((2, 3, CHUNK, 128), F32),
-            pltpu.VMEM((2, 3, PIECE, 128), F32),
+            pltpu.VMEM((4, 2, 3, PIECE, 128), F32),
             pltpu.VMEM((LAST, 2, 4, PIECE, 128), F32),
             pltpu.VMEM((LAST, 2, 2, 4, PIECE, 128), F32),
-            pltpu.VMEM((LAST, 2, 2, CUT, 128), F32),
-            pltpu.VMEM((LAST, 2, 2, PIECE, 128), F32),
             pltpu.VMEM((4, 256, 128), F32),
             pltpu.VMEM((4, 8, 32, 128), F32),
             pltpu.VMEM((512, 256), BF16),

time: 90.1 us -> 86.6 us (0.961)
  Pallas kernels: 87.5 us -> 84.1 us
    pallas_call x1, Pallas kernels: 87.5 us -> 84.1 us  [shards(): pl.pallas_call(kernel, out_shape=jax.ShapeDtypeStruct((64, 32, PIECE), F3...]
where the time goes in v3:
time: 86.6 us; the launch traced here: 86.3 us
  Pallas kernels  84.1 us (97%)
  local copies, waits for them, and re-layouts  2.26 us (3%)
    pallas_call x1, Pallas kernels, shards(): pl.pallas_call(kernel, out_shape=jax.ShapeDtypeStruct((64, 32, PIECE), F3...  84.1 us
    unnamed x1, local copies, waits for them, and re-layouts  2.26 us

profile of v3, /device:TPU:1, one launch (start us, length us, event | category | flops | bytes accessed | tf_op | source)
XLA Modules:
  0.0 86.3 jit_solution(5057998757438353834)
XLA Ops:
  0.0 84.1 %shard_map.55 = f32[64,32,104]{2,1,0:T(8,128)} custom-call(f32[2496,128]{1,0:T(8,128)} %bitcast.3, s32[2,39]{1,0:T(2,128)} %amp_tiles.1, f32[2496,1664]{1,0:T(8,128)} %ints.1, s32[26,39]{1,0:T(8,128)} %bitcast.4, f32[4,8,64]{2,1,0:T(8,128)} %bitcast.5), custom_call_target="tpu_custom_call" | custom-call | flops 26172456960 | bytes 18939904 | tf_op jit(solution)/shard_map/pallas_call | solution.py:462
  84.1 2.3 %copy.7 = f32[64,32,104]{2,1,0:T(8,128)} copy(f32[64,32,104]{2,1,0:T(8,128)} %shard_map.55) | data formatting | bytes 1703936
